TPU v7x, 32 devices: a whole 2x2x4 slice. The times are simulated.
32 devices in a mesh: ga: 2 (over x), gx: 8 (over z, y), yz: 2 (over core).
Axes of the slice: x: 2, y: 2, z: 4, core: 2. Of those that a mesh axis runs over, the one named last changes fastest.
Arguments:
- tokens: bfloat16 [2, 64, 18432], P(None, ('ga', 'gx'), 'yz'), parts along dimension 1, may hold values from -6 to 6
- norm_gain: bfloat16 [18432], P('yz'), may hold values from 0.099609375 to 1.8984375
- query_weight: bfloat16 [18432, 8192], P('yz', 'gx'), may hold values from -0.046875 to 0.046875
- kv_weight: bfloat16 [18432, 512], P('yz', 'gx'), may hold values from -0.046875 to 0.046875
- out_weight: bfloat16 [8192, 18432], P('gx', 'yz'), may hold values from -0.0625 to 0.0625
- cache: bfloat16 [64, 1024, 512], P(('ga', 'gx', 'yz')), parts along dimension 0, may hold values from -300 to 300
- cache_lengths: int32 [64], P(('ga', 'gx', 'yz')), parts along dimension 0, may hold values from 1 to 1024, as said below
Outputs:
- updated: bfloat16 [2, 64, 18432], P(None, ('ga', 'gx'), 'yz'), parts along dimension 1
There are 2 independent parts, one for each index of `ga`. A program takes and returns all parts, laid end to end along the dimension named above; an argument that names none is the same for every part. Nothing has to cross between parts.
Inputs may be any that keep to these rules, and one draw needn't show every extreme that they name: `cache_lengths`: some sequence has all 1024 slots filled.
All inputs are finite; a program needn't handle non-finite values.
Results may differ from a plain program's by a relative error of at most 0.0059.
Values may be sent and summed in bfloat16 or wider, within the bound.
A program may use at most 128 MiB of HBM per device.

v0:
```python
import jax
import jax.numpy as jnp
from jax import lax
from jax.sharding import PartitionSpec as P

D = 18432


def shards(tokens, norm_gain, query_weight, kv_weight, out_weight, cache, cache_lengths):
    steps_count = tokens.shape[0]
    row_count = tokens.shape[1]
    feature_cols = tokens.shape[2]
    head_cols = query_weight.shape[1]
    pair_cols = kv_weight.shape[1]
    groups = lax.axis_size("gx")
    seq_count = cache.shape[0]
    head_dim = cache.shape[2] // 2
    cache_slots = cache.shape[1]
    factor = head_dim ** (-0.5)
    filled = jnp.arange(cache_slots, dtype=jnp.int32)[None, :] < cache_lengths[:, None]
    pair_list = []
    results = []
    for step in range(steps_count):
        project_block = tokens[step : step + 1]
        step_count = project_block.shape[0]
        widened = project_block.reshape(step_count * row_count, feature_cols).astype(jnp.float32)
        totals = lax.psum((jnp.sum(widened, -1), jnp.sum(widened * widened, -1)), "yz")
        average = totals[0][:, None] / D
        spread = totals[1][:, None] / D - average * average
        scaled = (widened - average) * lax.rsqrt(spread + 1e-05) * norm_gain.astype(jnp.float32)
        normed = scaled.astype(jnp.bfloat16)
        piece = lax.all_gather(normed, "gx", axis=0, tiled=True)
        first = jnp.dot(piece, query_weight, preferred_element_type=jnp.float32)
        second = jnp.dot(piece, kv_weight, preferred_element_type=jnp.float32)
        partial_value = jnp.concatenate([first, second], 1)
        query_part = partial_value[:, :head_cols]
        pair_part = partial_value[:, head_cols:]
        query_moved = lax.all_to_all(query_part, "gx", split_axis=0, concat_axis=1, tiled=True)
        pair_moved = lax.all_to_all(pair_part, "gx", split_axis=0, concat_axis=1, tiled=True)
        query_sum = lax.psum_scatter(
            query_moved.reshape(step_count, row_count, groups * head_cols),
            "yz",
            scatter_dimension=1,
            tiled=True,
        )
        pair_sum = lax.psum_scatter(
            pair_moved.reshape(step_count, row_count, groups * pair_cols),
            "yz",
            scatter_dimension=1,
            tiled=True,
        )
        queries = query_sum.astype(jnp.bfloat16)
        new_pairs = pair_sum.astype(jnp.bfloat16)
        queries, new_pairs = (queries, new_pairs)
        pair_list.append(new_pairs[0])
        query = queries[0]
        fresh = jnp.stack(pair_list)
        head_count = query.shape[1] // head_dim
        query_heads = query.reshape(seq_count, head_count, head_dim)
        old_scores = (
            jnp.einsum(
                "bhd,bcd->bhc",
                query_heads,
                cache[:, :, :head_dim],
                preferred_element_type=jnp.float32,
            )
            * factor
        )
        old_scores = jnp.where(filled[:, None, :], old_scores, -jnp.inf)
        new_scores = (
            jnp.einsum(
                "bhd,sbd->bhs",
                query_heads,
                fresh[:, :, :head_dim],
                preferred_element_type=jnp.float32,
            )
            * factor
        )
        scores = jnp.concatenate([old_scores, new_scores], -1)
        highest = jnp.max(scores, -1, keepdims=True)
        raised = jnp.exp(scores - highest)
        weights = (raised / jnp.sum(raised, -1, keepdims=True)).astype(jnp.bfloat16)
        weighted = jnp.einsum(
            "bhc,bcd->bhd",
            weights[..., :cache_slots],
            cache[:, :, head_dim:],
            preferred_element_type=jnp.float32,
        )
        weighted = weighted + jnp.einsum(
            "bhs,sbd->bhd",
            weights[..., cache_slots:],
            fresh[:, :, head_dim:],
            preferred_element_type=jnp.float32,
        )
        attended = weighted.astype(jnp.bfloat16).reshape(seq_count, head_count * head_dim)
        output_attended = attended[None]
        by_sequence = jnp.transpose(output_attended, (1, 0, 2))
        group_rows = lax.all_gather(by_sequence, "yz", axis=0, tiled=True)
        per_head = lax.all_to_all(group_rows, "gx", split_axis=2, concat_axis=0, tiled=True)
        summed = lax.psum_scatter(
            jnp.einsum("rtk,kd->rtd", per_head, out_weight, preferred_element_type=jnp.float32),
            "gx",
            scatter_dimension=0,
            tiled=True,
        )
        results.append(
            (tokens[step : step + 1].astype(jnp.float32) + jnp.transpose(summed, (1, 0, 2))).astype(
                jnp.bfloat16
            )
        )
    return jnp.concatenate(results, 0)


def solution(mesh):
    in_specs = (
        P(None, ("ga", "gx"), "yz"),
        P("yz"),
        P("yz", "gx"),
        P("yz", "gx"),
        P("gx", "yz"),
        P(("ga", "gx", "yz"), None, None),
        P(("ga", "gx", "yz")),
    )
    out_specs = P(None, ("ga", "gx"), "yz")
    return jax.shard_map(shards, mesh=mesh, in_specs=in_specs, out_specs=out_specs, check_vma=False)
```

profile of v0, /device:TPU:0, one launch (start us, length us, event | category | flops | bytes accessed | tf_op | source)
XLA Modules:
  0.0 439.4 jit_solution(11016592627816897828)
XLA Ops:
  9.7 2.6 all-reduce.8
  13.3 33.2 %all-gather = bf16[8,4,9216]{2,1,0:T(4,128)(2,1)S(1)} all-gather(bf16[1,4,9216]{2,1,0:T(4,128)(2,1)S(1)} %get-tuple-element.19), channel_id=1, replica_groups=mesh['ga'=2,'gx'=8,'yz'=2] {'gx'}, dimensions={0}, use_global_device_ids=true | all-gather | bytes 663552 | tf_op jit(solution)/shard_map/all_gather | solution.py:32
  47.8 5.5 %all-to-all-start.1 = ((f32[8,1,256]{2,1,0:T(1,128)}), f32[8,1,256]{2,1,0:T(1,128)S(1)}, u32[]{:S(2)}, u32[]{:S(2)}) async-start(f32[8,1,256]{2,1,0:T(1,128)} %reshape.137), calls=%async_computation.1 | async-start | bytes 16384 | tf_op jit(solution)/shard_map/all_to_all | solution.py:39
  53.3 31.8 %all-gather.1 = bf16[8,4,9216]{2,1,0:T(4,128)(2,1)S(1)} all-gather(bf16[1,4,9216]{2,1,0:T(4,128)(2,1)S(1)} %get-tuple-element.20), channel_id=1, replica_groups=mesh['ga'=2,'gx'=8,'yz'=2] {'gx'}, dimensions={0}, use_global_device_ids=true | all-gather | bytes 663552 | tf_op jit(solution)/shard_map/all_gather | solution.py:32
  86.4 5.7 %all-to-all-start.4 = ((f32[8,1,256]{2,1,0:T(1,128)}), f32[8,1,256]{2,1,0:T(1,128)S(1)}, u32[]{:S(2)}, u32[]{:S(2)}) async-start(f32[8,1,256]{2,1,0:T(1,128)} %reshape.139), calls=%async_computation.4 | async-start | bytes 16384 | tf_op jit(solution)/shard_map/all_to_all | solution.py:39
  92.1 8.1 %fusion.49 = f32[32,1024]{1,0:T(8,128)S(1)} fusion(bf16[32,9216]{1,0:T(8,128)(2,1)S(1)} %reshape.116, bf16[9216,1024]{1,0:T(8,128)(2,1)} %param.9), kind=kOutput, calls=%fused_computation.88 | convolution fusion | flops 603979776 | bytes 19595264 | tf_op jit(solution)/shard_map/dot_general | solution.py:33
  100.8 6.0 %all-to-all-start = ((f32[8,4,1024]{2,1,0:T(4,128)}), f32[8,4,1024]{2,1,0:T(4,128)S(1)}, u32[]{:S(2)}, u32[]{:S(2)}) async-start(f32[8,4,1024]{2,1,0:T(4,128)} %all_to_all.70), calls=%async_computation | async-start | bytes 262144 | tf_op jit(solution)/shard_map/all_to_all | solution.py:38
  106.9 8.1 %fusion.51 = f32[32,1024]{1,0:T(8,128)S(1)} fusion(bf16[32,9216]{1,0:T(8,128)(2,1)S(1)} %reshape.118, bf16[9216,1024]{1,0:T(8,128)(2,1)} %param.9), kind=kOutput, calls=%fused_computation.90 | convolution fusion | flops 603979776 | bytes 19595264 | tf_op jit(solution)/shard_map/dot_general | solution.py:33
  115.6 6.0 %all-to-all-start.3 = ((f32[8,4,1024]{2,1,0:T(4,128)}), f32[8,4,1024]{2,1,0:T(4,128)S(1)}, u32[]{:S(2)}, u32[]{:S(2)}) async-start(f32[8,4,1024]{2,1,0:T(4,128)} %all_to_all.79), calls=%async_computation.3 | async-start | bytes 262144 | tf_op jit(solution)/shard_map/all_to_all | solution.py:38
  125.5 3.5 all-to-all-done.3
  129.0 4.6 %all-reduce.13 = (bf16[1,4,8192]{2,1,0:T(4,128)(2,1)S(1)}, bf16[1,4,512]{2,0,1:T(2,128)(2,1)S(1)}, bf16[1,4,512]{2,0,1:T(2,128)(2,1)S(1)}, bf16[1,4,8192]{2,1,0:T(4,128)(2,1)S(1)}) all-reduce(f32[1,4,8192]{2,1,0:T(4,128)S(1)} %bitcast.141, f32[1,4,512]{2,0,1:T(1,128)S(1)} %reshape.105, ...), channel_id=5, replica_groups=mesh['ga'=2,'gx'=8,'yz'=2] {'yz'}, use_global_device_ids=true, to_apply=%region_13.14.clone | all-reduce | flops 69632 | bytes 417792
  133.9 1.7 fusion.48
  135.6 1.7 fusion.46
  137.9 1.5 fusion.4
  139.6 2.1 all_gather.15
  142.2 6.8 %copy.39 = bf16[4,1,8192]{0,1,2:T(2,128)(2,1)} copy(bf16[4,1,8192]{2,1,0:T(2,128)(2,1)S(1)} %all_gather.15) | data formatting | bytes 131072 | tf_op jit(solution)/shard_map/all_gather | solution.py:98
  149.6 45.2 %reduce.10 = bf16[8192,4]{1,0:T(8,128)(2,1)S(1)} reduce(bf16[8192,1,4]{2,1,0:T(2,128)(2,1)} %bitcast.136, bf16[]{:T(256)} %broadcast.57), dimensions={1}, to_apply=%bitcast.109.reduce_sub_computation | reduce | bytes 131074
  194.8 4.6 %reshape.141 = bf16[8,2,2048]{2,1,0:T(2,128)(2,1)} reshape(bf16[8192,4]{1,0:T(8,128)(2,1)S(1)} %reduce.10) | data formatting | bytes 131072
  199.4 3.4 all-to-all-start.5
  202.7 1.5 fusion.2
  204.3 2.1 all_gather.13
  206.4 6.8 %copy.32 = bf16[4,1,8192]{0,1,2:T(2,128)(2,1)} copy(bf16[4,1,8192]{2,1,0:T(2,128)(2,1)S(1)} %all_gather.13) | data formatting | bytes 131072 | tf_op jit(solution)/shard_map/all_gather | solution.py:98
  213.2 45.2 %reduce.11 = bf16[8192,4]{1,0:T(8,128)(2,1)S(1)} reduce(bf16[8192,1,4]{2,1,0:T(2,128)(2,1)} %bitcast.137, bf16[]{:T(256)} %broadcast.57), dimensions={1}, to_apply=%bitcast.111.reduce_sub_computation | reduce | bytes 131074
  258.4 4.6 %reshape.143 = bf16[8,2,2048]{2,1,0:T(2,128)(2,1)} reshape(bf16[8192,4]{1,0:T(8,128)(2,1)S(1)} %reduce.11) | data formatting | bytes 131072
  263.0 5.9 %all-to-all-start.2 = ((bf16[8,2,2048]{2,1,0:T(2,128)(2,1)}), bf16[8,2,2048]{2,1,0:T(2,128)(2,1)S(1)}, u32[]{:S(2)}, u32[]{:S(2)}) async-start(bf16[8,2,2048]{2,1,0:T(2,128)(2,1)} %reshape.143), calls=%async_computation.2 | async-start | bytes 131072 | tf_op jit(solution)/shard_map/all_to_all | solution.py:99
  269.3 6.5 %reshape.142 = bf16[8192,1,4]{2,1,0:T(2,128)(2,1)} reshape(bf16[8,2,2048]{2,1,0:T(2,128)(2,1)S(1)} %all-to-all-done.5) | data formatting | bytes 131072
  275.8 8.1 %copy.40 = bf16[4,1,8192]{2,0,1:T(4,128)(2,1)S(1)} copy(bf16[4,1,8192]{0,1,2:T(2,128)(2,1)} %bitcast.138) | data formatting | bytes 131072 | tf_op jit(solution)/shard_map/all_to_all | solution.py:99
  284.0 6.5 %reshape.144 = bf16[8192,1,4]{2,1,0:T(2,128)(2,1)} reshape(bf16[8,2,2048]{2,1,0:T(2,128)(2,1)S(1)} %all-to-all-done.2) | data formatting | bytes 131072
  290.6 8.1 %copy.33 = bf16[4,1,8192]{2,0,1:T(4,128)(2,1)S(1)} copy(bf16[4,1,8192]{0,1,2:T(2,128)(2,1)} %bitcast.139) | data formatting | bytes 131072 | tf_op jit(solution)/shard_map/all_to_all | solution.py:99
  298.8 10.7 %convolution_bitcast_fusion = f32[32,1,9216]{2,0,1:T(8,128)} fusion(bf16[32,1024]{1,0:T(8,128)(2,1)S(1)} %reshape.112, bf16[1024,9216]{1,0:T(8,128)(2,1)} %param.11), kind=kOutput, calls=%fused_computation | convolution fusion | flops 603979776 | bytes 20119552 | tf_op jit(solution)/shard_map/rtk,kd->rtd/dot_general | solution.py:101
  309.5 10.8 %convolution_bitcast_fusion.1 = f32[32,1,9216]{2,0,1:T(8,128)} fusion(bf16[32,1024]{1,0:T(8,128)(2,1)S(1)} %reshape.109, bf16[1024,9216]{1,0:T(8,128)(2,1)} %param.11), kind=kOutput, calls=%fused_computation.1 | convolution fusion | flops 603979776 | bytes 20119552 | tf_op jit(solution)/shard_map/rtk,kd->rtd/dot_general | solution.py:101
  322.2 108.5 %all-reduce.12.cloned.1.call-done = (f32[32,1,9216]{2,0,1:T(8,128)}, f32[32,1,9216]{2,0,1:T(8,128)}) async-done(((f32[32,1,9216]{2,0,1:T(8,128)}, f32[32,1,9216]{2,0,1:T(8,128)}), (f32[32,1,9216]{2,0,1:T(8,128)}, f32[32,1,9216]{2,0,1:T(8,128)})) %all-reduce.12.cloned.1.call-update) | async-done | bytes 2359312
  (74 shorter events, 16.8 us)
Async XLA Ops:
  6.5 40.2 %copy-start = (bf16[9216,64]{0,1:T(8,128)(2,1)S(1)}, bf16[9216,64]{0,1:T(8,128)(2,1)}, u32[]{:S(2)}) copy-start(bf16[9216,64]{0,1:T(8,128)(2,1)} %param.10) | copy-start | bytes 3538948
  47.8 38.6 %all-to-all-start.1 = ((f32[8,1,256]{2,1,0:T(1,128)}), f32[8,1,256]{2,1,0:T(1,128)S(1)}, u32[]{:S(2)}, u32[]{:S(2)}) async-start(f32[8,1,256]{2,1,0:T(1,128)} %reshape.137), calls=%async_computation.1 | async-start | bytes 16384 | tf_op jit(solution)/shard_map/all_to_all | solution.py:39
  86.4 14.4 %all-to-all-start.4 = ((f32[8,1,256]{2,1,0:T(1,128)}), f32[8,1,256]{2,1,0:T(1,128)S(1)}, u32[]{:S(2)}, u32[]{:S(2)}) async-start(f32[8,1,256]{2,1,0:T(1,128)} %reshape.139), calls=%async_computation.4 | async-start | bytes 16384 | tf_op jit(solution)/shard_map/all_to_all | solution.py:39
  100.8 14.8 %all-to-all-start = ((f32[8,4,1024]{2,1,0:T(4,128)}), f32[8,4,1024]{2,1,0:T(4,128)S(1)}, u32[]{:S(2)}, u32[]{:S(2)}) async-start(f32[8,4,1024]{2,1,0:T(4,128)} %all_to_all.70), calls=%async_computation | async-start | bytes 262144 | tf_op jit(solution)/shard_map/all_to_all | solution.py:38
  106.8 14.8 %copy-start.6 = (u32[32]{0:T(128)S(1)}, u32[32]{0:T(128)}, u32[]{:S(2)}) copy-start(u32[32]{0:T(128)} %constant.21) | copy-start | bytes 388
  106.8 16.2 %copy-start.3 = (s32[2]{0:T(128)S(1)}, s32[2]{0:T(128)}, u32[]{:S(2)}) copy-start(s32[2]{0:T(128)} %param.13) | copy-start | bytes 28
  115.6 13.3 %all-to-all-start.3 = ((f32[8,4,1024]{2,1,0:T(4,128)}), f32[8,4,1024]{2,1,0:T(4,128)S(1)}, u32[]{:S(2)}, u32[]{:S(2)}) async-start(f32[8,4,1024]{2,1,0:T(4,128)} %all_to_all.79), calls=%async_computation.3 | async-start | bytes 262144 | tf_op jit(solution)/shard_map/all_to_all | solution.py:38
  199.4 63.6 %all-to-all-start.5 = ((bf16[8,2,2048]{2,1,0:T(2,128)(2,1)}), bf16[8,2,2048]{2,1,0:T(2,128)(2,1)S(1)}, u32[]{:S(2)}, u32[]{:S(2)}) async-start(bf16[8,2,2048]{2,1,0:T(2,128)(2,1)} %reshape.141), calls=%async_computation.5 | async-start | bytes 131072 | tf_op jit(solution)/shard_map/all_to_all | solution.py:99
  263.0 21.0 %all-to-all-start.2 = ((bf16[8,2,2048]{2,1,0:T(2,128)(2,1)}), bf16[8,2,2048]{2,1,0:T(2,128)(2,1)S(1)}, u32[]{:S(2)}, u32[]{:S(2)}) async-start(bf16[8,2,2048]{2,1,0:T(2,128)(2,1)} %reshape.143), calls=%async_computation.2 | async-start | bytes 131072 | tf_op jit(solution)/shard_map/all_to_all | solution.py:99
  269.0 161.7 %all-reduce.12.cloned.1.call-start = ((), (), s32[]{:S(2)}) async-start(), calls=%async_computation.6 | async-start | bytes 4718592
  309.5 123.0 %copy-start.1 = (bf16[9216,64]{0,1:T(8,128)(2,1)S(1)}, bf16[9216,64]{0,1:T(8,128)(2,1)}, u32[]{:S(2)}) copy-start(bf16[9216,64]{0,1:T(8,128)(2,1)} %param.10) | copy-start | bytes 3538948
  320.3 0.7 copy-start.5
  320.3 110.4 %copy-start.2 = (bf16[2,4,9216]{2,1,0:T(4,128)(2,1)S(1)}, bf16[2,4,9216]{2,1,0:T(4,128)(2,1)}, u32[]{:S(2)}) copy-start(bf16[2,4,9216]{2,1,0:T(4,128)(2,1)} %param.7) | copy-start | bytes 442372
  431.8 0.7 copy-start.4
Sparse Core Ops, SparseCore 0:
  320.5 110.1 all-reduce.11
where the time goes:
time: 441 us; the launch traced here: 439 us
  waiting for transfers between devices  112 us (25%)
  other arithmetic  98 us (22%)
  blocking collectives  76.5 us (17%)
  local copies, waits for them, and re-layouts  59.6 us (14%)
  matrix products  45.5 us (10%)
  starting transfers between devices  32.7 us (7%)
  between operations  15 us (3%)
    unnamed x2, waiting for transfers between devices  108 us
    unnamed x3, other arithmetic  91.5 us
    all_gather x2, blocking collectives, shards(): piece = lax.all_gather(normed, 'gx', axis=0, tiled=True)  65.1 us
    unnamed x30, local copies, waits for them, and re-layouts  27.2 us
    dot_general x2, matrix products, shards(): jnp.einsum('rtk,kd->rtd', per_head, out_weight, preferred_element_type=jn...  21.5 us
    all_to_all x4, local copies, waits for them, and re-layouts, shards(): lax.all_to_all(group_rows, 'gx', split_axis=2, concat_axis=0, tiled=True)  16.3 us
    dot_general x2, matrix products, shards(): first = jnp.dot(piece, query_weight, preferred_element_type=jnp.float32)  16.1 us
    all_gather x2, local copies, waits for them, and re-layouts, shards(): group_rows = lax.all_gather(by_sequence, 'yz', axis=0, tiled=True)  13.7 us
  transfers between devices with their start and end apart: 7, of which 2 were waited for; matrix products, arithmetic and copies ran while one was open for 21% of the time, Pallas kernels for 0%

commit v1 on v0

v1 whole, which is shorter than its diff:
```python
import functools

import jax
import jax.numpy as jnp
from jax import lax
from jax.experimental import pallas as pl
from jax.experimental.pallas import tpu as pltpu
from jax.sharding import PartitionSpec as P

BF = jnp.bfloat16
F32 = jnp.float32
TAIL = 128
PAIR = 2
LANES = 128


def up(n, m):
    return -(-n // m) * m


def iotas(shape):
    return lax.broadcasted_iota(jnp.int32, shape, 0), lax.broadcasted_iota(jnp.int32, shape, 1)


def pick(rows, cols, source):
    o, i = iotas((rows, cols))
    return jnp.where(source(o) == i, 1.0, 0.0).astype(BF)


def mm(a, b):
    return jnp.dot(a, b, preferred_element_type=F32)


def kernel(
    dims,
    lens, tok, gain, wq_h, wkv_h, wo_h, cache_h,
    out,
    wq, wkv, wo, ext, x32, st, st_r, xg, xall, acc, acc_r,
    qs, qr, kvs, kvr, ats, atr, att, own, ys, yr, zs, zr,
    w_sem, st_sem, ag_s, fw_s, ag_r, ac_sem, q_s, q_r, kv_s, kv_r, at_s, at_r, y_s, y_r, z_s, z_r,
):
    G, C, S, R, F, NB, HL, DH, KVC, CACHE, NC, QB = dims
    T = S * R
    Z = G // PAIR
    H = G * HL
    M = G * T
    fc = F // NC
    half = fc // 2
    W = S * NB
    QW = HL * DH
    g = lax.axis_index("gx")
    c = lax.axis_index("yz")
    z = g // PAIR
    y = g % PAIR
    yp = z * PAIR + (1 - y)

    for k in range(NC):
        rows = pl.ds(k * fc, fc)
        pltpu.make_async_copy(wq_h.at[rows], wq.at[rows], w_sem.at[k]).start()
    pltpu.make_async_copy(wkv_h, wkv, w_sem.at[NC]).start()
    for b in range(NB):
        pltpu.make_async_copy(cache_h.at[b], ext.at[b, pl.ds(0, CACHE)], w_sem.at[NC + 1 + b]).start()
    pltpu.make_async_copy(wo_h, wo, w_sem.at[NC + 1 + NB]).start()

    bar = pltpu.get_barrier_semaphore()
    n_dev = G * C
    me = g * C + c

    def greet(t, _):
        o = (me + t) % n_dev
        pl.semaphore_signal(bar, inc=1, device_id={"gx": o // C, "yz": o % C}, device_id_type=pl.DeviceIdType.MESH)
        return 0

    lax.fori_loop(1, n_dev, greet, 0)

    for s in range(S):
        x32[pl.ds(s * R, R), :] = tok[s].astype(F32)
    x = x32[...]
    st[0] = jnp.broadcast_to(jnp.sum(x, -1, keepdims=True), (T, LANES))
    st[1] = jnp.broadcast_to(jnp.sum(x * x, -1, keepdims=True), (T, LANES))
    pl.semaphore_wait(bar, n_dev - 1)

    def rcopy(src, dst, ss, rs, dev):
        return pltpu.make_async_remote_copy(
            src_ref=src, dst_ref=dst, send_sem=ss, recv_sem=rs, device_id=dev, device_id_type=pl.DeviceIdType.MESH
        )

    st_copy = rcopy(st, st_r, st_sem.at[0], st_sem.at[1], {"yz": 1 - c})
    st_copy.start()
    for b in range(NB):
        ext[b, pl.ds(CACHE, TAIL), :] = jnp.zeros((TAIL, 2 * DH), BF)
    acc[...] = jnp.zeros_like(acc)
    st_copy.wait()
    D = F * C
    average = ((st[0] + st_r[0]) / D)[:, :1]
    spread = ((st[1] + st_r[1]) / D)[:, :1] - average * average
    inv = lax.rsqrt(spread + 1e-05)

    def ag(k, t):
        dev = yp if t == 0 else ((z + t) % Z) * PAIR + y
        return rcopy(xg.at[k, g], xg.at[k, g], ag_s.at[k, t], ag_r.at[k, g], {"gx": dev})

    def fw(k, t):
        o = ((z + t) % Z) * PAIR + y
        return rcopy(xg.at[k, o], xg.at[k, o], fw_s.at[k, t], ag_r.at[k, o], {"gx": yp})

    for k in range(NC):
        parts = []
        for p in range(2):
            cols = pl.ds(k * fc + p * half, half)
            parts.append((x32[:, cols] - average) * inv * gain[:, cols].astype(F32))
        xg[k, g] = jnp.concatenate(parts, 0).astype(BF)
        for t in range(1, Z):
            ag(k, t).start()
        ag(k, 0).start()

    for k in range(NC):
        for t in range(1, Z):
            o = ((z + t) % Z) * PAIR + y
            rcopy(xg.at[k, o], xg.at[k, o], fw_s.at[k, t], ag_r.at[k, o], {"gx": yp}).wait_recv()
            fw(k, t).start()

    for k in range(NC):
        for t in range(Z):
            o = ((z + t) % Z) * PAIR + (1 - y)
            rcopy(xg.at[k, o], xg.at[k, o], fw_s.at[k, t], ag_r.at[k, o], {"gx": yp}).wait_recv()
        rows = pl.ds(k * fc, fc)
        for p in range(2):
            block = xg[k].astype(F32)[:, p * T:(p + 1) * T, :].reshape(M, half)
            xall[:, pl.ds(k * fc + p * half, half)] = block.astype(BF)
        pltpu.make_async_copy(wq_h.at[rows], wq.at[rows], w_sem.at[k]).wait()
        if k == 0:
            pltpu.make_async_copy(wkv_h, wkv, w_sem.at[NC]).wait()

        def project(n, _):
            cols = pl.ds(pl.multiple_of(n * DH, DH), DH)
            acc[:, cols] += mm(xall[:, rows], wq[rows, cols])
            return 0

        lax.fori_loop(0, HL, project, 0)
        acc[:, pl.ds(QW, KVC)] += mm(xall[:, rows], wkv[rows, :])

    ac = rcopy(acc, acc_r, ac_sem.at[0], ac_sem.at[1], {"yz": 1 - c})
    ac.start()
    ac.wait()

    def from_w(o, width):
        return o // width, o % width

    def q_source(o):
        d, w = from_w(o, QB)
        hl, s, b = w // W, (w // NB) % S, w % NB
        return jnp.where(w < HL * W, hl * M + d * T + s * R + c * NB + b, -1)

    def kv_source(o):
        d, w = from_w(o, 16)
        return jnp.where(w < W, d * T + (w // NB) * R + c * NB + w % NB, -1)

    kv_all = (acc[:, pl.ds(QW, LANES)] + acc_r[:, pl.ds(QW, LANES)]).astype(BF)
    kvs[...] = mm(pick(G * 16, M, kv_source), kv_all).astype(BF).reshape(G, 16, LANES)
    q_all = jnp.concatenate(
        [(acc[:, pl.ds(n * DH, DH)] + acc_r[:, pl.ds(n * DH, DH)]).astype(BF) for n in range(HL)], 0
    )
    qs[...] = mm(pick(G * QB, HL * M, q_source), q_all).astype(BF).reshape(G, QB, DH)

    def q_copy(t):
        o = (g + t) % G
        return rcopy(qs.at[o], qr.at[g], q_s.at[t], q_r.at[g], {"gx": o})

    def kv_copy(t):
        o = (g + t) % G
        return rcopy(kvs.at[o], kvr.at[g], kv_s.at[t], kv_r.at[g], {"gx": o})

    def q_start(t, _):
        kv_copy(t).start()
        q_copy(t).start()
        return 0

    lax.fori_loop(1, G, q_start, 0)
    kvr[g] = kvs[g]
    qr[g] = qs[g]

    def q_wait(t, _):
        o = (g + t) % G
        rcopy(kvs.at[o], kvr.at[o], kv_s.at[t], kv_r.at[o], {"gx": o}).wait_recv()
        rcopy(qs.at[o], qr.at[o], q_s.at[t], q_r.at[o], {"gx": o}).wait_recv()
        return 0

    lax.fori_loop(1, G, q_wait, 0)

    fresh = jnp.zeros((16, 2 * DH), F32)
    for d in range(G):
        i, n = iotas((LANES, 2 * DH))
        spread_cols = jnp.where((i < KVC) & (n == i + d * KVC), 1.0, 0.0).astype(BF)
        fresh = fresh + mm(kvr[d], spread_cols)
    fresh = fresh.astype(BF)
    for b in range(NB):
        rows_b = mm(pick(16, 16, lambda o: jnp.where(o < S, o * NB + b, -1)), fresh)
        ext[b, pl.ds(CACHE, 16), :] = rows_b.astype(BF)

    HS = H * S

    def r_source(o):
        b, h, s = o // HS, (o // S) % H, o % S
        return (h // HL) * QB + (h % HL) * W + s * NB + b

    query = mm(pick(NB * HS, G * QB, r_source), qr[...].reshape(G * QB, DH)).astype(BF)
    slots = CACHE + TAIL
    factor = DH ** (-0.5)
    outs = []
    for b in range(NB):
        pltpu.make_async_copy(cache_h.at[b], ext.at[b, pl.ds(0, CACHE)], w_sem.at[NC + 1 + b]).wait()
        qb = query[b * HS:(b + 1) * HS]
        scores = lax.dot_general(
            qb, ext[b, :, pl.ds(0, DH)], (((1,), (1,)), ((), ())), preferred_element_type=F32
        ) * factor
        row, slot = iotas((HS, slots))
        seen = (slot < lens[b]) | ((slot >= CACHE) & (slot - CACHE <= row % S))
        scores = jnp.where(seen, scores, -jnp.inf)
        raised = jnp.exp(scores - jnp.max(scores, -1, keepdims=True))
        weights = (raised / jnp.sum(raised, -1, keepdims=True)).astype(BF)
        outs.append(mm(weights, ext[b, :, pl.ds(DH, DH)]).astype(BF))
    attended = jnp.concatenate(outs, 0)

    def a_source(o):
        d, w = from_w(o, QB)
        hl, s, b = w // W, (w // NB) % S, w % NB
        return jnp.where(w < HL * W, b * HS + (d * HL + hl) * S + s, -1)

    ats[...] = mm(pick(G * QB, NB * HS, a_source), attended).astype(BF).reshape(G, QB, DH)

    def at_copy(t):
        o = (me + t) % n_dev
        return rcopy(ats.at[o // C], atr.at[me], at_s.at[t], at_r.at[me], {"gx": o // C, "yz": o % C})

    def at_start(t, _):
        at_copy(t).start()
        return 0

    lax.fori_loop(1, n_dev, at_start, 0)
    atr[me] = ats[g]

    def at_wait(t, _):
        o = (me + t) % n_dev
        rcopy(ats.at[o // C], atr.at[o], at_s.at[t], at_r.at[o], {"gx": o // C, "yz": o % C}).wait_recv()
        return 0

    lax.fori_loop(1, n_dev, at_wait, 0)

    ZT = Z * T

    def o_source(o):
        hl, r = from_w(o, M)
        rel, line, u = r // ZT, (r // T) % Z, r % T
        s, d, b = u // R, (u % R) // NB, u % NB
        dev = line * PAIR + jnp.where(rel == 0, y, 1 - y)
        return (dev * C + d) * QB + hl * W + s * NB + b

    ordered = mm(pick(HL * M, n_dev * QB, o_source), atr[...].reshape(n_dev * QB, DH)).astype(BF)
    for n in range(HL):
        att[:, pl.ds(n * DH, DH)] = ordered[n * M:(n + 1) * M]
    pltpu.make_async_copy(wo_h, wo, w_sem.at[NC + 1 + NB]).wait()

    tile = 256
    def y_copy(k):
        return rcopy(ys.at[k], yr.at[k], y_s.at[k], y_r.at[k], {"gx": yp})

    for k in range(NC):
        def project_out(n, _):
            at = pl.multiple_of(n * tile, tile)
            part = mm(att[...], wo[:, pl.ds(k * fc + at, tile)])
            own[:, pl.ds(k * fc + at, tile)] = part[:ZT]
            ys[k, :, pl.ds(at, tile)] = part[ZT:].astype(BF)
            return 0

        lax.fori_loop(0, fc // tile, project_out, 0)
        y_copy(k).start()

    def z_copy(k, t):
        o = (z + t) % Z
        return rcopy(zs.at[k, o], zr.at[k, z], z_s.at[k, t], z_r.at[k, z], {"gx": o * PAIR + y})

    for k in range(NC):
        y_copy(k).wait_recv()
        cols = pl.ds(k * fc, fc)
        own[:, cols] += yr[k].astype(F32)

        for t in range(1, Z):
            o = (z + t) % Z
            r = pl.ds(pl.multiple_of(o * T, T), T)
            parts = [own[r, pl.ds(k * fc + p * half, half)] for p in range(2)]
            zs[k, o] = jnp.concatenate(parts, 0).astype(BF)
            z_copy(k, t).start()

    for k in range(NC):
        total = []
        r = pl.ds(pl.multiple_of(z * T, T), T)
        for p in range(2):
            total.append(own[r, pl.ds(k * fc + p * half, half)])
        total = jnp.concatenate(total, 0)
        for t in range(1, Z):
            o = (z + t) % Z
            rcopy(zs.at[k, o], zr.at[k, o], z_s.at[k, t], z_r.at[k, o], {"gx": yp}).wait_recv()
            total = total + zr[k, o].astype(F32)
        for p in range(2):
            cols = pl.ds(k * fc + p * half, half)
            res = (total[p * T:(p + 1) * T] + x32[:, cols]).astype(BF)
            for s in range(S):
                out[s, :, cols] = res[s * R:(s + 1) * R]

    for k in range(NC):
        ag(k, 0).wait_send()
        y_copy(k).wait_send()
        for t in range(1, Z):
            ag(k, t).wait_send()
            fw(k, t).wait_send()
            z_copy(k, t).wait_send()

    def q_sent(t, _):
        kv_copy(t).wait_send()
        q_copy(t).wait_send()
        return 0

    lax.fori_loop(1, G, q_sent, 0)

    def at_sent(t, _):
        at_copy(t).wait_send()
        return 0

    lax.fori_loop(1, n_dev, at_sent, 0)


def shards(tokens, norm_gain, query_weight, kv_weight, out_weight, cache, cache_lengths):
    S, R, F = tokens.shape
    G = lax.axis_size("gx")
    C = lax.axis_size("yz")
    NB, CACHE, two = cache.shape
    DH = two // 2
    HL = query_weight.shape[1] // DH
    KVC = kv_weight.shape[1]
    NC = 4
    T = S * R
    Z = G // PAIR
    M = G * T
    fc = F // NC
    half = fc // 2
    QB = up(HL * S * NB, 16)
    NDEV = G * C
    dims = (G, C, S, R, F, NB, HL, DH, KVC, CACHE, NC, QB)
    V = pltpu.VMEM
    dma = pltpu.SemaphoreType.DMA
    width = HL * DH + LANES
    scratch = [
        V((F, HL * DH), BF), V((F, KVC), BF), V((HL * DH, F), BF), V((NB, CACHE + TAIL, two), BF),
        V((T, F), F32), V((2, T, LANES), F32), V((2, T, LANES), F32),
        V((NC, G, 2 * T, half), BF), V((M, F), BF), V((M, width), F32), V((M, width), F32),
        V((G, QB, DH), BF), V((G, QB, DH), BF), V((G, 16, LANES), BF), V((G, 16, LANES), BF),
        V((G, QB, DH), BF), V((NDEV, QB, DH), BF), V((M, HL * DH), BF),
        V((Z * T, F), F32), V((NC, Z * T, fc), BF), V((NC, Z * T, fc), BF),
        V((NC, Z, 2 * T, half), BF), V((NC, Z, 2 * T, half), BF),
        dma((NC + 2 + NB,)), dma((2,)), dma((NC, Z)), dma((NC, Z)), dma((NC, G)), dma((2,)),
        dma((G,)), dma((G,)), dma((G,)), dma((G,)), dma((NDEV,)), dma((NDEV,)),
        dma((NC,)), dma((NC,)), dma((NC, Z)), dma((NC, Z)),
    ]
    vm = pl.BlockSpec(memory_space=pltpu.VMEM)
    hbm = pl.BlockSpec(memory_space=pl.ANY)
    return pl.pallas_call(
        functools.partial(kernel, dims),
        out_shape=jax.ShapeDtypeStruct(tokens.shape, BF),
        in_specs=[pl.BlockSpec(memory_space=pltpu.SMEM), vm, vm, hbm, hbm, hbm, hbm],
        out_specs=vm,
        scratch_shapes=scratch,
        compiler_params=pltpu.CompilerParams(
            collective_id=0, has_side_effects=True, vmem_limit_bytes=58 * 1024 * 1024
        ),
        name="layer",
    )(cache_lengths, tokens, norm_gain.reshape(1, F), query_weight, kv_weight, out_weight, cache)


def solution(mesh):
    in_specs = (
        P(None, ("ga", "gx"), "yz"),
        P("yz"),
        P("yz", "gx"),
        P("yz", "gx"),
        P("gx", "yz"),
        P(("ga", "gx", "yz"), None, None),
        P(("ga", "gx", "yz")),
    )
    out_specs = P(None, ("ga", "gx"), "yz")
    return jax.shard_map(shards, mesh=mesh, in_specs=in_specs, out_specs=out_specs, check_vma=False)
```

time: 441 us -> 74 us (0.17)
  waiting for transfers between devices: 112 us -> 0 us
  other arithmetic: 98 us -> 0 us
  blocking collectives: 76.5 us -> 0 us
  Pallas kernels: 0 us -> 67 us
  local copies, waits for them, and re-layouts: 59.6 us -> 6.68 us
  matrix products: 45.5 us -> 0 us
  starting transfers between devices: 32.7 us -> 0 us
  between operations: 15 us -> 0.01 us
    unnamed x2 -> x0, waiting for transfers between devices: 108 us -> none
    unnamed x3 -> x0, other arithmetic: 91.5 us -> none
    all_gather x4 -> x0, blocking collectives: 69.3 us -> none  [the longest x2 65.1 us: shards(): piece = lax.all_gather(normed, 'gx', axis=0, tiled=True)]
    pallas_call x0 -> x1, Pallas kernels: none -> 67 us  [shards(): pl.pallas_call(functools.partial(kernel, dims), out_shape=jax.ShapeDtypeS...]
    dot_general x13 -> x0, matrix products: 45.5 us -> none  [the longest x2 21.5 us: shards(): jnp.einsum('rtk,kd->rtd', per_head, out_weight, preferred_element_type=jn...]
    all_to_all x6 -> x0, starting transfers between devices: 32.4 us -> none  [the longest x2 12 us: shards(): lax.all_to_all(query_part, 'gx', split_axis=0, concat_axis=1, tiled=True)]
    unnamed x30 -> x2, local copies, waits for them, and re-layouts: 27.2 us -> 5.32 us
    all_to_all x9 -> x0, local copies, waits for them, and re-layouts: 18.3 us -> none  [the longest x4 16.3 us: shards(): lax.all_to_all(group_rows, 'gx', split_axis=2, concat_axis=0, tiled=True)]
  transfers between devices with their start and end apart: 7 -> 0, of which waited for: 2 -> 0; matrix products, arithmetic and copies ran while one was open for 21% -> 0% of each run, Pallas kernels for 0% -> 0%
where the time goes in v1:
time: 74 us; the launch traced here: 73.7 us
  Pallas kernels  67 us (91%)
  local copies, waits for them, and re-layouts  6.68 us (9%)
    pallas_call x1, Pallas kernels, shards(): pl.pallas_call(functools.partial(kernel, dims), out_shape=jax.ShapeDtypeS...  67 us
    unnamed x2, local copies, waits for them, and re-layouts  5.32 us

profile of v1, /device:TPU:0, one launch (start us, length us, event | category | flops | bytes accessed | tf_op | source)
XLA Modules:
  0.0 73.7 jit_solution(2042415181763471150)
XLA Ops:
  0.0 1.4 %reshape.3.gain = bf16[1,9216]{1,0:T(2,128)(2,1)} reshape(bf16[9216]{0:T(1024)(128)(2,1)} %param.8) | data formatting | bytes 36864 | tf_op jit(solution)/shard_map/reshape | solution.py:377
  1.4 3.7 %copy.8.wkv_h = bf16[9216,64]{1,0:T(8,128)(2,1)} copy(bf16[9216,64]{0,1:T(8,128)(2,1)} %param.10) | data formatting | bytes 2359296 | tf_op args[3]
  5.1 67.0 %layer.1 = bf16[2,4,9216]{2,1,0:T(4,128)(2,1)} custom-call(s32[2]{0:T(128)} %lens.1, bf16[2,4,9216]{2,1,0:T(4,128)(2,1)} %tok.1, bf16[1,9216]{1,0:T(2,128)(2,1)} %reshape.3.gain, bf16[9216,1024]{1,0:T(8,128)(2,1)} %wq_h.1, bf16[9216,64]{1,0:T(8,128)(2,1)} %copy.8.wkv_h, bf16[1024,9216]{1,0:T(8,128)(2,1)} %wo_h.1, bf16[2,1024,512]{2,1,0:T(8,128)(2,1)} %cache_h.1), custom_call_target="tpu_custom_call" | custom-call | tf_op jit(solution)/shard_map/layer/pallas_call | solution.py:367
  72.1 1.6 %copy.10 = bf16[2,4,9216]{2,1,0:T(4,128)(2,1)} copy(bf16[2,4,9216]{2,1,0:T(4,128)(2,1)} %layer.1) | data formatting | bytes 294912

commit v2 on v1

--- a/solution.py
+++ b/solution.py
@@ -104,11 +104,14 @@
         o = ((z + t) % Z) * PAIR + y
         return rcopy(xg.at[k, o], xg.at[k, o], fw_s.at[k, t], ag_r.at[k, o], {"gx": yp})
 
+    gains = gain[...].astype(F32)
     for k in range(NC):
         parts = []
         for p in range(2):
             cols = pl.ds(k * fc + p * half, half)
-            parts.append((x32[:, cols] - average) * inv * gain[:, cols].astype(F32))
+            first = (k * fc + p * half) // LANES
+            row = jnp.concatenate([gains[first + i:first + i + 1] for i in range(half // LANES)], 1)
+            parts.append((x32[:, cols] - average) * inv * row)
         xg[k, g] = jnp.concatenate(parts, 0).astype(BF)
         for t in range(1, Z):
             ag(k, t).start()
@@ -138,7 +141,9 @@
             return 0
 
         lax.fori_loop(0, HL, project, 0)
-        acc[:, pl.ds(QW, KVC)] += mm(xall[:, rows], wkv[rows, :])
+        acc[:, pl.ds(QW, KVC)] += lax.dot_general(
+            xall[:, rows], wkv[:, rows], (((1,), (1,)), ((), ())), preferred_element_type=F32
+        )
 
     ac = rcopy(acc, acc_r, ac_sem.at[0], ac_sem.at[1], {"yz": 1 - c})
     ac.start()
@@ -351,7 +356,7 @@
     dma = pltpu.SemaphoreType.DMA
     width = HL * DH + LANES
     scratch = [
-        V((F, HL * DH), BF), V((F, KVC), BF), V((HL * DH, F), BF), V((NB, CACHE + TAIL, two), BF),
+        V((F, HL * DH), BF), V((KVC, F), BF), V((HL * DH, F), BF), V((NB, CACHE + TAIL, two), BF),
         V((T, F), F32), V((2, T, LANES), F32), V((2, T, LANES), F32),
         V((NC, G, 2 * T, half), BF), V((M, F), BF), V((M, width), F32), V((M, width), F32),
         V((G, QB, DH), BF), V((G, QB, DH), BF), V((G, 16, LANES), BF), V((G, 16, LANES), BF),
@@ -374,7 +379,7 @@
             collective_id=0, has_side_effects=True, vmem_limit_bytes=58 * 1024 * 1024
         ),
         name="layer",
-    )(cache_lengths, tokens, norm_gain.reshape(1, F), query_weight, kv_weight, out_weight, cache)
+    )(cache_lengths, tokens, norm_gain.reshape(F // LANES, LANES), query_weight, kv_weight.T, out_weight, cache)
 
 
 def solution(mesh):

time: 74 us -> 68.8 us (0.930)
  local copies, waits for them, and re-layouts: 6.68 us -> 1.62 us
    unnamed x2 -> x1, local copies, waits for them, and re-layouts: 5.32 us -> 1.62 us
    reshape x1 -> x0, local copies, waits for them, and re-layouts: 1.36 us -> none  [shards(): norm_gain.reshape(1, F)]
where the time goes in v2:
time: 68.8 us; the launch traced here: 68.6 us
  Pallas kernels  67 us (97%)
  local copies, waits for them, and re-layouts  1.62 us (2%)
    pallas_call x1, Pallas kernels, shards(): pl.pallas_call(functools.partial(kernel, dims), out_shape=jax.ShapeDtypeS...  67 us
    unnamed x1, local copies, waits for them, and re-layouts  1.62 us

profile of v2, /device:TPU:0, one launch (start us, length us, event | category | flops | bytes accessed | tf_op | source)
XLA Modules:
  0.0 68.6 jit_solution(10456504879850233065)
XLA Ops:
  0.0 67.0 %layer.1 = bf16[2,4,9216]{2,1,0:T(4,128)(2,1)} custom-call(s32[2]{0:T(128)} %lens.1, bf16[2,4,9216]{2,1,0:T(4,128)(2,1)} %tok.1, bf16[72,128]{1,0:T(8,128)(2,1)} %bitcast.3, bf16[9216,1024]{1,0:T(8,128)(2,1)} %wq_h.1, bf16[64,9216]{1,0:T(8,128)(2,1)} %bitcast.2, bf16[1024,9216]{1,0:T(8,128)(2,1)} %wo_h.1, bf16[2,1024,512]{2,1,0:T(8,128)(2,1)} %cache_h.1), custom_call_target="tpu_custom_call" | custom-call | tf_op jit(solution)/shard_map/layer/pallas_call | solution.py:372
  67.0 1.6 %copy.9 = bf16[2,4,9216]{2,1,0:T(4,128)(2,1)} copy(bf16[2,4,9216]{2,1,0:T(4,128)(2,1)} %layer.1) | data formatting | bytes 294912
